TPU v7x, 128 devices: a whole 4x4x4 slice. The times are simulated.
128 devices in a mesh: gx: 8 (over x_hi, z), gy: 16 (over y, x_lo, core).
Axes of the slice: x: 4 (x_hi: 2, x_lo: 2; x = x_hi * 2 + x_lo), y: 4, z: 4, core: 2. Of those that a mesh axis runs over, the one named last changes fastest.
Arguments:
- die_basis: float32 [128, 512, 512], P('gx', 'gy'), may hold values from -0.0390625 to 0.0390625
- die_coeff: float32 [5, 128, 512], P(None, 'gx', 'gy'), may hold values from 0.2 to 5
- pkg_basis: float32 [4096, 64, 512], P(('gx', 'gy')), may hold values from -0.09375 to 0.09375
- send_blocks: int32 [128, 4, 4], P(('gx', 'gy')), may hold values from 0 to 31
- columns: int32 [5, 4096, 4], P(None, ('gx', 'gy')), may hold values from 0 to 47
- counts: int32 [5, 4096], P(None, ('gx', 'gy')), may hold values from 1 to 4
- pkg_blocks: float32 [5, 4096, 64, 256], P(None, ('gx', 'gy')), may hold values from -48 to 48
Outputs:
- reduced: float32 [5, 512, 512], replicated
Inputs may be any that keep to these rules, and one draw needn't show every extreme that they name: `columns`: indices below 32 name the partition's own blocks, the others its ghost blocks in the order of the statement.
All inputs are finite; a program needn't handle non-finite values.
Results may differ from a plain program's by a relative error of at most 0.0001.
Values sent between devices are 32-bit elements; how exact they have to be, the bound alone decides.
A program may use at most 256 MiB of HBM per device.

v0:
```python
import jax
import jax.numpy as jnp
from jax import lax
from jax.sharding import PartitionSpec as P

highest = lax.Precision.HIGHEST


def from_behind(value, axis, steps):
    count = lax.axis_size(axis)
    leading, last = (max(0, -steps), min(count, count - steps))
    return lax.ppermute(value, axis, [(source, source + steps) for source in range(leading, last)])


def passed_along(value, axis, steps):
    count = lax.axis_size(axis)
    pairs = [(source, (source + steps) % count) for source in range(count)]
    return lax.ppermute(value, axis, pairs)


def weighted_gram(weights, field):
    width = field.shape[-1]
    flat = field.reshape(-1, width)
    scaled = weights.reshape(-1, 1) * flat
    return lax.dot_general(
        flat,
        scaled,
        (((0,), (0,)), ((), ())),
        precision=highest,
        preferred_element_type=jnp.float32,
    )


def die_terms(basis, coeff, next_x_row, next_y_col):
    next_x = jnp.concatenate([basis[1:], next_x_row], axis=0)
    next_y = jnp.concatenate([basis[:, 1:], next_y_col], axis=1)
    diff_x = basis - next_x
    diff_y = basis - next_y
    return jnp.stack(
        [
            weighted_gram(coeff[0], basis),
            weighted_gram(coeff[1], diff_x),
            weighted_gram(coeff[2], diff_y),
            weighted_gram(coeff[3], basis),
            weighted_gram(coeff[4], diff_x) + weighted_gram(coeff[4], diff_y),
        ]
    )


def package_terms(owned, table, columns, counts, blocks):
    row_count = owned.shape[0]
    block = owned.shape[1]
    width = owned.shape[2]
    entries = columns.shape[-1]
    results = []
    for term_idx in range(columns.shape[0]):
        picked = table[columns[term_idx]]
        live = (jnp.arange(entries, dtype=jnp.int32)[None, :] < counts[term_idx][:, None]).astype(
            jnp.float32
        )
        matrices = (
            blocks[term_idx].reshape(row_count, block, entries, block) * live[:, None, :, None]
        )
        image = jnp.einsum("rinj,rnjk->rik", matrices, picked, precision=highest)
        results.append(
            lax.dot_general(
                owned.reshape(-1, width),
                image.reshape(-1, width),
                (((0,), (0,)), ((), ())),
                precision=highest,
                preferred_element_type=jnp.float32,
            )
        )
    return jnp.stack(results)


def body(die_basis, die_coeff, pkg_basis, send_blocks, columns, counts, pkg_blocks):
    next_x_row = from_behind(die_basis[:1], "gx", -1)
    next_y_col = from_behind(die_basis[:, :1], "gy", -1)
    lists = send_blocks[0]
    from_lower_x = passed_along(pkg_basis[lists[0]], "gx", 1)
    from_upper_x = passed_along(pkg_basis[lists[1]], "gx", -1)
    from_lower_y = passed_along(pkg_basis[lists[2]], "gy", 1)
    from_upper_y = passed_along(pkg_basis[lists[3]], "gy", -1)
    table = jnp.concatenate(
        [pkg_basis, from_lower_x, from_upper_x, from_lower_y, from_upper_y], axis=0
    )
    partial_terms = die_terms(die_basis, die_coeff, next_x_row, next_y_col)
    partial_terms = partial_terms + package_terms(pkg_basis, table, columns, counts, pkg_blocks)
    return lax.psum(partial_terms, ("gx", "gy"))


def solution(mesh):
    placed = (
        P("gx", "gy", None),
        P(None, "gx", "gy"),
        P(("gx", "gy"), None, None),
        P(("gx", "gy"), None, None),
        P(None, ("gx", "gy"), None),
        P(None, ("gx", "gy")),
        P(None, ("gx", "gy"), None, None),
    )
    return jax.shard_map(body, mesh=mesh, in_specs=placed, out_specs=P(), check_vma=False)
```

profile of v0, /device:TPU:1, one launch (start us, length us, event | category | flops | bytes accessed | tf_op | source)
XLA Modules:
  0.0 471.7 jit_solution(8393592863045458205)
XLA Ops:
  7.4 3.6 gather_fusion
  11.0 2.5 collective-permute-start.2
  13.4 3.6 gather_fusion.1
  17.0 4.6 collective-permute-start.3
  21.6 3.6 gather_fusion.2
  26.4 3.6 gather_fusion.3
  30.0 5.5 %collective-permute-start.1 = (f32[16,1,512]{2,1,0:T(1,128)S(1)}, f32[16,1,512]{2,1,0:T(1,128)S(1)}, u32[]{:S(2)}, u32[]{:S(2)}) collective-permute-start(f32[16,1,512]{2,1,0:T(1,128)S(1)} %slice.94), channel_id=1, source_target_pairs={{1,0},{2,1},{3,2},{4,3},{5,4},{6,5},{7,6},{8,7},{9,8},{10,9},{11,1... | collective-permute-start | bytes 98312 | tf_op jit(solution)/shard_map/ppermute | solution.py:12
  35.5 4.9 %constant_dynamic-update-slice_fusion.4 = f32[48,64,512]{2,1,0:T(8,128)} fusion(f32[32,64,512]{2,1,0:T(8,128)} %param.9), kind=kLoop, calls=%fused_computation.81 | loop fusion | bytes 8388608
  40.8 7.9 %fusion.120 = (f32[1,32,64,256]{3,2,1,0:T(8,128)S(1)}, f32[1,32,64,256]{3,2,1,0:T(8,128)}, f32[1,32,64,256]{3,2,1,0:T(8,128)}, f32[1,32,64,256]{3,2,1,0:T(8,128)}, f32[1,32,64,256]{3,2,1,0:T(8,128)}) fusion(f32[5,32,64,256]{3,2,1,0:T(8,128)} %param.13), kind=kLoop, calls=%fused_computation.128 | loop fusion | bytes 20971520 | tf_op jit(solution)/shard_map/slice | solution.py:62
  48.8 5.1 %reshape_squeeze.22 = f32[32,64,4,64]{3,2,1,0:T(4,128)} reshape(f32[1,32,64,256]{3,2,1,0:T(8,128)} %get-tuple-element.7) | data formatting | bytes 4194304 | tf_op jit(solution)/shard_map/reshape;squeeze | solution.py:62
  54.0 5.1 %reshape_squeeze.10 = f32[32,64,4,64]{3,2,1,0:T(4,128)} reshape(f32[1,32,64,256]{3,2,1,0:T(8,128)} %get-tuple-element.8) | data formatting | bytes 4194304 | tf_op jit(solution)/shard_map/reshape;squeeze | solution.py:62
  59.1 5.1 %reshape_squeeze.23 = f32[32,64,4,64]{3,2,1,0:T(4,128)} reshape(f32[1,32,64,256]{3,2,1,0:T(8,128)} %get-tuple-element.6) | data formatting | bytes 4194304 | tf_op jit(solution)/shard_map/reshape;squeeze | solution.py:62
  64.5 5.1 %reshape_squeeze.24 = f32[32,64,4,64]{3,2,1,0:T(4,128)} reshape(f32[1,32,64,256]{3,2,1,0:T(8,128)} %get-tuple-element.9) | data formatting | bytes 4194304 | tf_op jit(solution)/shard_map/reshape;squeeze | solution.py:62
  69.6 3.3 reshape_squeeze.25
  73.0 2.0 fusion.35
  75.1 2.9 broadcast_multiply_fusion.3
  78.0 2.9 broadcast_multiply_fusion.4
  81.1 2.9 broadcast_multiply_fusion.2
  84.0 2.9 broadcast_multiply_fusion.1
  87.0 3.0 broadcast_multiply_fusion
  91.7 2.2 fusion.59
  94.0 1.9 collective-permute-done
  95.9 2.1 fusion.41
  98.0 2.2 fusion.47
  100.3 2.0 fusion.53
  102.2 2.2 fusion.98
  104.5 2.3 copy-done.10
  108.7 1.9 constant_dynamic-update-slice_fusion.2
  110.6 1.9 constant_dynamic-update-slice_fusion.1
  112.5 1.9 constant_dynamic-update-slice_fusion
  114.3 13.1 %gather_fusion.5 = f32[128,64,512]{2,1,0:T(8,128)} fusion(f32[48,64,512]{2,1,0:T(8,128)} %constant_dynamic-update-slice_fusion, s32[1024]{0:T(1024)S(1)} %get-tuple-element.32), kind=kCustom, calls=%fused_computation.5 | custom fusion | bytes 33554944 | tf_op jit(solution)/shard_map/gather | solution.py:57
  127.5 12.7 %gather_fusion.4 = f32[128,64,512]{2,1,0:T(8,128)} fusion(f32[48,64,512]{2,1,0:T(8,128)} %constant_dynamic-update-slice_fusion, s32[1024]{0:T(1024)S(1)} %pad_clamp_fusion.4), kind=kCustom, calls=%fused_computation.4 | custom fusion | bytes 33554944 | tf_op jit(solution)/shard_map/gather | solution.py:57
  140.1 13.7 %fusion.18 = f32[32,64,512,1]{2,1,3,0:T(8,128)S(1)} fusion(f32[32,4,64,512]{3,2,1,0:T(8,128)} %bitcast.211, f32[32,64,4,64]{3,2,1,0:T(4,128)} %broadcast_multiply_fusion.4), kind=kOutput, calls=%fused_computation.27 | convolution fusion | flops 3221225472 | bytes 23068672 | tf_op jit(solution)/shard_map/rinj,rnjk->rik/dot_general | solution.py:64
  153.9 8.0 %fusion.65 = f32[5,512,512]{1,2,0:T(8,128)} fusion(f32[32,64,512]{2,1,0:T(8,128)S(1)} %copy-done.9, f32[32,64,512,1]{2,1,3,0:T(8,128)S(1)} %fusion.18), kind=kOutput, calls=%fused_computation.57 | convolution fusion | flops 6442450944 | bytes 9437184 | tf_op jit(solution)/shard_map/dot_general | solution.py:66
  161.9 12.7 %gather_fusion.6 = f32[128,64,512]{2,1,0:T(8,128)} fusion(f32[48,64,512]{2,1,0:T(8,128)} %constant_dynamic-update-slice_fusion, s32[1024]{0:T(1024)S(1)} %get-tuple-element.31), kind=kCustom, calls=%fused_computation.6 | custom fusion | bytes 33554944 | tf_op jit(solution)/shard_map/gather | solution.py:57
  174.5 12.6 %gather_fusion.7 = f32[128,64,512]{2,1,0:T(8,128)} fusion(f32[48,64,512]{2,1,0:T(8,128)} %constant_dynamic-update-slice_fusion, s32[1024]{0:T(1024)S(1)} %get-tuple-element.30), kind=kCustom, calls=%fused_computation.7 | custom fusion | bytes 33554944 | tf_op jit(solution)/shard_map/gather | solution.py:57
  187.2 12.9 %gather_fusion.8 = f32[128,64,512]{2,1,0:T(8,128)} fusion(f32[48,64,512]{2,1,0:T(8,128)} %constant_dynamic-update-slice_fusion, s32[1024]{0:T(1024)S(1)} %get-tuple-element.29), kind=kCustom, calls=%fused_computation.8 | custom fusion | bytes 33554944 | tf_op jit(solution)/shard_map/gather | solution.py:57
  200.0 16.1 %fusion.16 = f32[32,64,512,1]{2,1,3,0:T(8,128)} fusion(f32[32,4,64,512]{3,2,1,0:T(8,128)} %bitcast.206, f32[32,64,4,64]{3,2,1,0:T(4,128)} %broadcast_multiply_fusion.3), kind=kOutput, calls=%fused_computation.25 | convolution fusion | flops 3221225472 | bytes 23068672 | tf_op jit(solution)/shard_map/rinj,rnjk->rik/dot_general | solution.py:64
  216.1 10.4 %fusion.71 = f32[5,512,512]{1,2,0:T(8,128)} fusion(f32[5,512,512]{1,2,0:T(8,128)} %fusion.65, f32[32,64,512]{2,1,0:T(8,128)} %param.9, f32[32,64,512,1]{2,1,3,0:T(8,128)} %fusion.16), kind=kOutput, calls=%fused_computation.59 | convolution fusion | flops 6442450944 | bytes 9437184 | tf_op jit(solution)/shard_map/dot_general | solution.py:66
  226.5 12.2 %fusion.14 = f32[32,64,512,1]{2,1,3,0:T(8,128)} fusion(f32[32,4,64,512]{3,2,1,0:T(8,128)S(1)} %bitcast.210, f32[32,64,4,64]{3,2,1,0:T(4,128)S(1)} %copy-done.6), kind=kOutput, calls=%fused_computation.23 | convolution fusion | flops 3221225472 | bytes 23068672 | tf_op jit(solution)/shard_map/rinj,rnjk->rik/dot_general | solution.py:64
  238.8 10.4 %fusion.77 = f32[5,512,512]{1,2,0:T(8,128)} fusion(f32[5,512,512]{1,2,0:T(8,128)} %fusion.71, f32[32,64,512]{2,1,0:T(8,128)} %param.9, f32[32,64,512,1]{2,1,3,0:T(8,128)} %fusion.14), kind=kOutput, calls=%fused_computation.61 | convolution fusion | flops 6442450944 | bytes 9437184 | tf_op jit(solution)/shard_map/dot_general | solution.py:66
  249.2 14.7 %fusion.12 = f32[32,64,512,1]{2,1,3,0:T(8,128)} fusion(f32[32,4,64,512]{3,2,1,0:T(8,128)} %bitcast.207, f32[32,64,4,64]{3,2,1,0:T(4,128)S(1)} %copy-done.8), kind=kOutput, calls=%fused_computation.21 | convolution fusion | flops 3221225472 | bytes 23068672 | tf_op jit(solution)/shard_map/rinj,rnjk->rik/dot_general | solution.py:64
  263.9 10.5 %fusion.83 = f32[5,512,512]{1,2,0:T(8,128)} fusion(f32[5,512,512]{1,2,0:T(8,128)} %fusion.77, f32[32,64,512]{2,1,0:T(8,128)} %param.9, f32[32,64,512,1]{2,1,3,0:T(8,128)} %fusion.12), kind=kOutput, calls=%fused_computation.63 | convolution fusion | flops 6442450944 | bytes 9437184 | tf_op jit(solution)/shard_map/dot_general | solution.py:66
  274.4 11.8 %fusion.10 = f32[32,64,512,1]{2,1,3,0:T(8,128)} fusion(f32[32,4,64,512]{3,2,1,0:T(8,128)S(1)} %bitcast.205, f32[32,64,4,64]{3,2,1,0:T(4,128)S(1)} %copy-done.7), kind=kOutput, calls=%fused_computation.19 | convolution fusion | flops 3221225472 | bytes 23068672 | tf_op jit(solution)/shard_map/rinj,rnjk->rik/dot_general | solution.py:64
  286.2 10.2 %fusion.89 = f32[5,512,512]{1,2,0:T(8,128)} fusion(f32[5,512,512]{1,2,0:T(8,128)} %fusion.83, f32[32,64,512]{2,1,0:T(8,128)} %param.9, f32[32,64,512,1]{2,1,3,0:T(8,128)} %fusion.10), kind=kOutput, calls=%fused_computation.65 | convolution fusion | flops 6442450944 | bytes 9437184 | tf_op jit(solution)/shard_map/dot_general | solution.py:66
  296.5 7.9 %add.108 = f32[5,512,512]{1,2,0:T(8,128)} add(f32[5,512,512]{1,2,0:T(8,128)} %copy-done.10, f32[5,512,512]{1,2,0:T(8,128)} %fusion.89) | non-fusion elementwise | flops 1310720 | bytes 15728640 | tf_op jit(solution)/shard_map/add | solution.py:89
  304.4 154.3 %all-reduce.2.cloned.1.call-done = f32[5,512,512]{1,2,0:T(8,128)} async-done(((f32[5,512,512]{1,2,0:T(8,128)}), f32[5,512,512]{1,2,0:T(8,128)}) %all-reduce.2.cloned.1.call-update) | async-done | bytes 5242896 | tf_op jit(solution)/shard_map/psum | solution.py:90
  458.7 5.9 %copy.27 = f32[5,512,512]{2,1,0:T(8,128)} copy(f32[5,512,512]{1,2,0:T(8,128)} %all-reduce.2.cloned.1.call-done) | data formatting | bytes 10485760 | tf_op jit(solution)/shard_map/psum | solution.py:90
  (84 shorter events, 7.1 us)
Async XLA Ops:
  6.5 23.4 %copy-start = (f32[16,32,512]{2,1,0:T(8,128)S(1)}, f32[16,32,512]{2,1,0:T(8,128)}, u32[]{:S(2)}) copy-start(f32[16,32,512]{2,1,0:T(8,128)} %param.7) | copy-start | bytes 3145732
  6.5 452.2 %all-reduce.2.cloned.1.call-start = ((), (), s32[]{:S(2)}) async-start(), calls=%async_computation | async-start | bytes 10485760 | tf_op jit(solution)/shard_map/psum | solution.py:90
  11.0 95.8 %collective-permute-start.2 = (f32[4,64,512]{2,1,0:T(8,128)}, f32[4,64,512]{2,1,0:T(8,128)}, u32[]{:S(2)}, u32[]{:S(2)}) collective-permute-start(f32[4,64,512]{2,1,0:T(8,128)} %gather_fusion), channel_id=1, source_target_pairs={{0,16},{16,32},{32,48},{48,64},{64,80},{80,96},{96,112},{112,0},{1... | collective-permute-start | bytes 1572872 | tf_op jit(solution)/shard_map/ppermute | solution.py:18
  17.0 91.7 %collective-permute-start.3 = (f32[4,64,512]{2,1,0:T(8,128)}, f32[4,64,512]{2,1,0:T(8,128)}, u32[]{:S(2)}, u32[]{:S(2)}) collective-permute-start(f32[4,64,512]{2,1,0:T(8,128)} %gather_fusion.1), channel_id=1, source_target_pairs={{0,112},{16,0},{32,16},{48,32},{64,48},{80,64},{96,80},{112,96},{1... | collective-permute-start | bytes 1572872 | tf_op jit(solution)/shard_map/ppermute | solution.py:18
  25.2 85.4 %collective-permute-start.4 = (f32[4,64,512]{2,1,0:T(8,128)}, f32[4,64,512]{2,1,0:T(8,128)}, u32[]{:S(2)}, u32[]{:S(2)}) collective-permute-start(f32[4,64,512]{2,1,0:T(8,128)} %gather_fusion.2), channel_id=1, source_target_pairs={{0,1},{1,2},{2,3},{3,4},{4,5},{5,6},{6,7},{7,8},{8,9},{9,10},{10,1... | collective-permute-start | bytes 1572872 | tf_op jit(solution)/shard_map/ppermute | solution.py:18
  29.9 82.5 %collective-permute-start.5 = (f32[4,64,512]{2,1,0:T(8,128)}, f32[4,64,512]{2,1,0:T(8,128)}, u32[]{:S(2)}, u32[]{:S(2)}) collective-permute-start(f32[4,64,512]{2,1,0:T(8,128)} %gather_fusion.3), channel_id=1, source_target_pairs={{0,15},{1,0},{2,1},{3,2},{4,3},{5,4},{6,5},{7,6},{8,7},{9,8},{10,9... | collective-permute-start | bytes 1572872 | tf_op jit(solution)/shard_map/ppermute | solution.py:18
  30.0 10.4 %copy-start.12 = (s32[5,32,4]{1,2,0:T(4,128)S(1)}, s32[5,32,4]{1,2,0:T(4,128)}, u32[]{:S(2)}) copy-start(s32[5,32,4]{1,2,0:T(4,128)} %param.11) | copy-start | bytes 7684
  30.0 10.8 %copy-start.13 = (s32[5,32]{1,0:T(8,128)S(1)}, s32[5,32]{1,0:T(8,128)}, u32[]{:S(2)}) copy-start(s32[5,32]{1,0:T(8,128)} %param.12) | copy-start | bytes 1924
  30.0 60.2 %collective-permute-start.1 = (f32[16,1,512]{2,1,0:T(1,128)S(1)}, f32[16,1,512]{2,1,0:T(1,128)S(1)}, u32[]{:S(2)}, u32[]{:S(2)}) collective-permute-start(f32[16,1,512]{2,1,0:T(1,128)S(1)} %slice.94), channel_id=1, source_target_pairs={{1,0},{2,1},{3,2},{4,3},{5,4},{6,5},{7,6},{8,7},{9,8},{10,9},{11,1... | collective-permute-start | bytes 98312 | tf_op jit(solution)/shard_map/ppermute | solution.py:12
  69.6 3.4 copy-start.11
  72.9 2.2 copy-start.4
  75.1 2.9 copy-start.5
  78.0 3.0 copy-start.1
  81.1 3.0 copy-start.2
  84.0 2.9 copy-start.3
  90.2 5.7 %collective-permute-start = (f32[1,32,512]{2,1,0:T(8,128)S(1)}, f32[1,32,512]{2,1,0:T(8,128)S(1)}, u32[]{:S(2)}, u32[]{:S(2)}) collective-permute-start(f32[1,32,512]{2,1,0:T(8,128)S(1)} %slice.91), channel_id=1, source_target_pairs={{16,0},{32,16},{48,32},{64,48},{80,64},{96,80},{112,96},{17,1},{33... | collective-permute-start | bytes 196616 | tf_op jit(solution)/shard_map/ppermute | solution.py:12
  104.4 2.4 copy-start.10
  140.1 13.7 %copy-start.9 = (f32[32,64,512]{2,1,0:T(8,128)S(1)}, f32[32,64,512]{2,1,0:T(8,128)}, u32[]{:S(2)}) copy-start(f32[32,64,512]{2,1,0:T(8,128)} %param.9) | copy-start | bytes 12582916
  200.0 26.5 %slice-start.4 = ((s8[16777216]{0:T(1024)(128)(4,1)}), s8[4194304]{0:T(1024)(128)(4,1)S(1)}, s32[]{:S(2)}) async-start(s8[16777216]{0:T(1024)(128)(4,1)} %bitcast.208), calls=%async_computation.5 | async-start | bytes 8388608
  200.0 26.5 %slice-start.5 = ((s8[16777216]{0:T(1024)(128)(4,1)}), s8[4194304]{0:T(1024)(128)(4,1)S(1)}, s32[]{:S(2)}) async-start(s8[16777216]{0:T(1024)(128)(4,1)} %bitcast.208), calls=%async_computation.6 | async-start | bytes 8388608
  200.0 26.5 %slice-start.6 = ((s8[16777216]{0:T(1024)(128)(4,1)}), s8[4194304]{0:T(1024)(128)(4,1)S(1)}, s32[]{:S(2)}) async-start(s8[16777216]{0:T(1024)(128)(4,1)} %bitcast.208), calls=%async_computation.7 | async-start | bytes 8388608
  216.1 10.4 %slice-start.7 = ((s8[16777216]{0:T(1024)(128)(4,1)}), s8[4194304]{0:T(1024)(128)(4,1)S(1)}, s32[]{:S(2)}) async-start(s8[16777216]{0:T(1024)(128)(4,1)} %bitcast.208), calls=%async_computation.8 | async-start | bytes 8388608
  216.1 10.4 %copy-start.6 = (f32[32,64,4,64]{3,2,1,0:T(4,128)S(1)}, f32[32,64,4,64]{3,2,1,0:T(4,128)}, u32[]{:S(2)}) copy-start(f32[32,64,4,64]{3,2,1,0:T(4,128)} %broadcast_multiply_fusion.2) | copy-start | bytes 6291460
  238.8 10.4 %copy-start.8 = (f32[32,64,4,64]{3,2,1,0:T(4,128)S(1)}, f32[32,64,4,64]{3,2,1,0:T(4,128)}, u32[]{:S(2)}) copy-start(f32[32,64,4,64]{3,2,1,0:T(4,128)} %broadcast_multiply_fusion.1) | copy-start | bytes 6291460
  249.1 25.2 %slice-start = ((s8[16777216]{0:T(1024)(128)(4,1)}), s8[4194304]{0:T(1024)(128)(4,1)S(1)}, s32[]{:S(2)}) async-start(s8[16777216]{0:T(1024)(128)(4,1)} %bitcast.203), calls=%async_computation.1 | async-start | bytes 8388608
  249.1 25.2 %slice-start.1 = ((s8[16777216]{0:T(1024)(128)(4,1)}), s8[4194304]{0:T(1024)(128)(4,1)S(1)}, s32[]{:S(2)}) async-start(s8[16777216]{0:T(1024)(128)(4,1)} %bitcast.203), calls=%async_computation.2 | async-start | bytes 8388608
  249.2 25.2 %slice-start.2 = ((s8[16777216]{0:T(1024)(128)(4,1)}), s8[4194304]{0:T(1024)(128)(4,1)S(1)}, s32[]{:S(2)}) async-start(s8[16777216]{0:T(1024)(128)(4,1)} %bitcast.203), calls=%async_computation.3 | async-start | bytes 8388608
  263.9 10.5 %slice-start.3 = ((s8[16777216]{0:T(1024)(128)(4,1)}), s8[4194304]{0:T(1024)(128)(4,1)S(1)}, s32[]{:S(2)}) async-start(s8[16777216]{0:T(1024)(128)(4,1)} %bitcast.203), calls=%async_computation.4 | async-start | bytes 8388608
  263.9 10.5 %copy-start.7 = (f32[32,64,4,64]{3,2,1,0:T(4,128)S(1)}, f32[32,64,4,64]{3,2,1,0:T(4,128)}, u32[]{:S(2)}) copy-start(f32[32,64,4,64]{3,2,1,0:T(4,128)} %broadcast_multiply_fusion) | copy-start | bytes 6291460
Sparse Core Ops, SparseCore 0:
  304.6 154.1 all-reduce.1
where the time goes:
time: 480 us; the launch traced here: 472 us
  waiting for transfers between devices  156 us (32%)
  local copies, waits for them, and re-layouts  132 us (28%)
  matrix products  131 us (27%)
  other arithmetic  23.7 us (5%)
  starting transfers between devices  15.3 us (3%)
  between operations  13.9 us (3%)
    psum x1, waiting for transfers between devices, body(): return lax.psum(partial_terms, ('gx', 'gy'))  154 us
    dot_general x5, matrix products, package_terms(): image = jnp.einsum('rinj,rnjk->rik', matrices, picked, precision=highest)  68.5 us
    gather x5, local copies, waits for them, and re-layouts, package_terms(): picked = table[columns[term_idx]]  64 us
    dot_general x5, matrix products, package_terms(): lax.dot_general(owned.reshape(-1, width), image.reshape(-1, width), (((0,...  49.5 us
    another operation x5, local copies, waits for them, and re-layouts, package_terms(): blocks[term_idx].reshape(row_count, block, entries, block)  23.5 us
    mul x5, other arithmetic, package_terms(): blocks[term_idx].reshape(row_count, block, entries, block)  14.7 us
    unnamed x48, local copies, waits for them, and re-layouts  13 us
    dot_general x6, matrix products, weighted_gram(): lax.dot_general(flat, scaled, (((0,), (0,)), ((), ())), precision=highest...  12.7 us
  transfers between devices with their start and end apart: 7, of which 2 were waited for; matrix products, arithmetic and copies ran while one was open for 17% of the time, Pallas kernels for 0%

commit v1 on v0

v1 whole, which is shorter than its diff:
```python
import jax
import jax.numpy as jnp
from jax import lax
from jax.experimental import pallas as pl
from jax.experimental.pallas import tpu as pltpu
from jax.sharding import PartitionSpec as P

MESH = pl.DeviceIdType.MESH
f32 = jnp.float32
bf16 = jnp.bfloat16
TERMS = 5
HALF = 1024
SHARE = (256, 64, 16)


def split(value):
    high = value.astype(bf16)
    low = (value - high.astype(f32)).astype(bf16)
    return high, low


def dot3(left, right):
    return jnp.dot(
        jnp.concatenate([left[0], left[1], left[0]], axis=1),
        jnp.concatenate([right[0], right[0], right[1]], axis=0),
        preferred_element_type=f32,
    )


def kernel(
    die, coeff, basis, lists, columns, counts, blocks, out,
    table, basis_t, staged, image, total, field_t, field, share, summed,
    ghost_out, ghost_in, row_in, col_out, col_in, got_core, got_0, got_1, got_2,
    ghost_send, ghost_recv, halo_send, halo_recv, stage_sem, out_sem, send_sem, recv_sem,
):
    gx, gy = lax.axis_index("gx"), lax.axis_index("gy")
    core = lax.rem(gy, 2)
    spot = ((gx // 4) * 2 + lax.rem(gy // 2, 2), gy // 4, lax.rem(gx, 4))
    got = (got_0, got_1, got_2)

    def device_at(x, y, z, on_core):
        return ((x // 2) * 4 + z, y * 4 + lax.rem(x, 2) * 2 + on_core)

    def which(axis):
        return ((2 - axis) * (1 - axis) // 2, axis * (2 - axis), axis * (axis - 1) // 2)

    def along(axis, steps):
        x, y, z = (lax.rem(s + steps * w, 4) for s, w in zip(spot, which(axis)))
        return device_at(x, y, z, core)

    def place_on(axis):
        return sum(s * w for s, w in zip(spot, which(axis)))

    sibling = device_at(*spot, 1 - core)
    around = (
        (lax.rem(gx + 1, 8), gy),
        (lax.rem(gx + 7, 8), gy),
        (gx, lax.rem(gy + 1, 16)),
        (gx, lax.rem(gy + 15, 16)),
    )

    def stage_copy(half_term, slot):
        term, half = half_term // 2, lax.rem(half_term, 2)
        return pltpu.make_async_copy(
            blocks.at[term, pl.ds(half * 16, 16)], staged.at[slot], stage_sem.at[slot]
        )

    stage_copy(0, 0).start()

    barrier = pltpu.get_barrier_semaphore()
    partners = [along(axis, steps) for axis in range(3) for steps in (1, 2, 3)]
    partners += [sibling, *around]
    for partner in partners:
        pl.semaphore_signal(barrier, inc=1, device_id=partner, device_id_type=MESH)
    pl.semaphore_wait(barrier, len(partners))

    def remote(source, target, send, recv, device):
        return pltpu.make_async_remote_copy(
            src_ref=source, dst_ref=target, send_sem=send, recv_sem=recv,
            device_id=device, device_id_type=MESH,
        )

    row_copy = remote(die.at[0], row_in, halo_send.at[0], halo_recv.at[0], around[1])
    row_copy.start()
    col_out[...] = die[:, 0, :]
    col_copy = remote(col_out, col_in, halo_send.at[1], halo_recv.at[1], around[3])
    col_copy.start()
    ghost_copies = []
    for side in range(4):
        for slot in range(4):
            ghost_out[side, slot] = basis[lists[0, side, slot]]
        copy = remote(
            ghost_out.at[side], ghost_in.at[side], ghost_send.at[side], ghost_recv.at[side],
            around[side],
        )
        copy.start()
        ghost_copies.append(copy)

    def prepare(group, carry):
        value = basis[pl.ds(group * 4, 4)].reshape(256, 512)
        high, low = split(value)
        table[0, pl.ds(group * 4, 4)] = high.reshape(4, 64, 512)
        table[1, pl.ds(group * 4, 4)] = low.reshape(4, 64, 512)
        high, low = split(value.T)
        basis_t[group, 0] = high
        basis_t[group, 1] = low
        return carry

    lax.fori_loop(0, 8, prepare, 0)

    own = die[...]
    row_copy.wait()
    col_copy.wait()
    next_row = jnp.where(gx == 7, 0.0, row_in[...])
    next_col = jnp.where(gy == 15, 0.0, col_in[...])

    def keep_field(index, value):
        flat = value.reshape(512, 512)
        high, low = split(flat)
        field[index, 0] = high
        field[index, 1] = low
        field_t[index] = flat.T

    keep_field(0, own)
    keep_field(1, own - jnp.concatenate([own[1:], next_row[None]], axis=0))
    last = lax.broadcasted_iota(jnp.int32, (16, 32, 512), 1) == 31
    keep_field(2, own - jnp.where(last, next_col[:, None, :], jnp.roll(own, -1, axis=1)))
    share[...] = jnp.zeros_like(share)

    def die_term(step, carry):
        index = step // 2
        odd = lax.rem(step, 2)
        term = (1 - odd) * index + odd * (3 + (index + 1) // 2)
        weighted = split(field_t[index] * coeff[pl.ds(term, 1), :])
        gram = dot3(weighted, (field[index, 0], field[index, 1]))
        for lane in range(4):
            share[term, lane * 512 : (lane + 1) * 512] += gram[:, lane * 128 : (lane + 1) * 128]
        return carry

    lax.fori_loop(0, 6, die_term, 0)

    for side in range(4):
        ghost_copies[side].wait()
        high, low = split(ghost_in[side])
        table[0, 32 + side * 4 : 36 + side * 4] = high
        table[1, 32 + side * 4 : 36 + side * 4] = low

    lane_at = lax.broadcasted_iota(jnp.int32, (64, 256), 1)

    def half_term(at):
        term, half, slot = at // 2, lax.rem(at, 2), lax.rem(at, 2)
        stage_copy(at, slot).wait()

        @pl.when(at < 2 * TERMS - 1)
        def _():
            stage_copy(at + 1, 1 - slot).start()

        for step in range(16):
            row = half * 16 + step
            kept = jnp.where(lane_at < counts[term, row] * 64, staged[slot, step], 0.0)
            high, low = split(kept)
            picks = [columns[term, row, entry] for entry in range(4)]
            picked_high = jnp.concatenate([table[0, pick] for pick in picks], axis=0)
            picked_low = jnp.concatenate([table[1, pick] for pick in picks], axis=0)
            both = jnp.dot(
                jnp.concatenate([high, low], axis=0), picked_high, preferred_element_type=f32
            )
            value = both[:64] + both[64:] + jnp.dot(high, picked_low, preferred_element_type=f32)
            high, low = split(value)
            image[0, step * 64 : (step + 1) * 64] = high
            image[1, step * 64 : (step + 1) * 64] = low
        highs = [basis_t[half * 4 + part, 0] for part in range(4)]
        lows = [basis_t[half * 4 + part, 1] for part in range(4)]
        product = jnp.dot(
            jnp.concatenate(highs + lows + highs, axis=1),
            jnp.concatenate([image[0], image[0], image[1]], axis=0),
            preferred_element_type=f32,
        )
        for lane in range(4):
            share[term, lane * 512 : (lane + 1) * 512] += product[:, lane * 128 : (lane + 1) * 128]

    def offset(term, level):
        start = core * HALF
        for i in range(level):
            start = start + place_on(lax.rem(term + i, 3)) * SHARE[i]
        return pl.multiple_of(start, 16)

    def wait_bytes(ref, sem):
        pltpu.make_async_copy(ref, ref, sem).wait()

    def core_send(term):
        there = pl.multiple_of((1 - core) * HALF, 16)
        remote(
            share.at[term, pl.ds(there, HALF)], got_core.at[term],
            send_sem.at[term, 0], recv_sem.at[term, 0], sibling,
        ).start()

    def core_add(term):
        wait_bytes(got_core.at[term], recv_sem.at[term, 0])
        share[term, pl.ds(offset(term, 0), HALF)] += got_core[term]

    def scatter(term, level):
        axis, base, rows = lax.rem(term + level, 3), offset(term, level), SHARE[level]
        for steps in (1, 2, 3):
            there = pl.multiple_of(base + lax.rem(place_on(axis) + steps, 4) * rows, 16)
            remote(
                share.at[term, pl.ds(there, rows)],
                got[level].at[term, pl.ds((steps - 1) * rows, rows)],
                send_sem.at[term, 1 + level], recv_sem.at[term, 1 + level], along(axis, steps),
            ).start()

    def add(term, level, target):
        wait_bytes(got[level].at[term], recv_sem.at[term, 1 + level])
        rows, here = SHARE[level], pl.ds(offset(term, level + 1), SHARE[level])
        target[term, here] = (
            share[term, here]
            + got[level][term, :rows]
            + got[level][term, rows : 2 * rows]
            + got[level][term, 2 * rows :]
        )

    def gather(term, level):
        here = pl.ds(offset(term, level + 1), SHARE[level])
        axis = lax.rem(term + level, 3)
        for steps in (1, 2, 3):
            remote(
                summed.at[term, here], summed.at[term, here],
                send_sem.at[term, 4 + level], recv_sem.at[term, 4 + level], along(axis, steps),
            ).start()

    def gathered(term, level):
        wait_bytes(got[level].at[term], recv_sem.at[term, 4 + level])

    def core_gather(term):
        here = pl.ds(offset(term, 0), HALF)
        remote(
            summed.at[term, here], summed.at[term, here],
            send_sem.at[term, 7], recv_sem.at[term, 7], sibling,
        ).start()

    def write(term):
        wait_bytes(got_core.at[term], recv_sem.at[term, 7])
        for lane in range(4):
            pltpu.make_async_copy(
                summed.at[term, pl.ds(lane * 512, 512)],
                out.at[term, :, pl.ds(lane * 128, 128)],
                out_sem.at[term],
            ).start()

    def stage_0(term):
        core_send(term)

    def stage_1(term):
        core_add(term)
        scatter(term, 0)

    def stage_2(term):
        add(term, 0, share)
        scatter(term, 1)

    def stage_3(term):
        add(term, 1, share)
        scatter(term, 2)

    def stage_4(term):
        add(term, 2, summed)
        gather(term, 2)

    def stage_5(term):
        gathered(term, 2)
        gather(term, 1)

    def stage_6(term):
        gathered(term, 1)
        gather(term, 0)

    def stage_7(term):
        gathered(term, 0)
        core_gather(term)

    stages = (stage_0, stage_1, stage_2, stage_3, stage_4, stage_5, stage_6, stage_7, write)

    def turn(at, carry):
        @pl.when(at < 2 * TERMS)
        def _():
            half_term(at)

        for k in reversed(range(len(stages))):
            since = at - 1 - k
            term = since // 2

            @pl.when((since >= 0) & (since < 2 * TERMS) & (lax.rem(since + 20, 2) == 0))
            def _(k=k, term=term):
                stages[k](term)

        return carry

    lax.fori_loop(0, 2 * TERMS + 8, turn, 0)

    def finish(term, carry):
        for k in (0, 7):
            wait_bytes(got_core.at[term], send_sem.at[term, k])
        for level in range(3):
            wait_bytes(got[level].at[term], send_sem.at[term, 1 + level])
            wait_bytes(got[level].at[term], send_sem.at[term, 4 + level])
        wait_bytes(summed.at[term], out_sem.at[term])
        return carry

    lax.fori_loop(0, TERMS, finish, 0)


def body(die_basis, die_coeff, pkg_basis, send_blocks, columns, counts, pkg_blocks):
    vmem = pl.BlockSpec(memory_space=pltpu.VMEM)
    smem = pl.BlockSpec(memory_space=pltpu.SMEM)
    anywhere = pl.BlockSpec(memory_space=pl.ANY)
    dma = pltpu.SemaphoreType.DMA
    return pl.pallas_call(
        kernel,
        out_shape=jax.ShapeDtypeStruct((TERMS, 512, 512), f32),
        in_specs=[vmem, vmem, vmem, smem, smem, smem, anywhere],
        out_specs=anywhere,
        scratch_shapes=[
            pltpu.VMEM((2, 48, 64, 512), bf16),
            pltpu.VMEM((8, 2, 512, 256), bf16),
            pltpu.VMEM((2, 16, 64, 256), f32),
            pltpu.VMEM((2, 1024, 512), bf16),
            pltpu.VMEM((8, 128), f32),
            pltpu.VMEM((3, 512, 512), f32),
            pltpu.VMEM((3, 2, 512, 512), bf16),
            pltpu.VMEM((TERMS, 2 * HALF, 128), f32),
            pltpu.VMEM((TERMS, 2 * HALF, 128), f32),
            pltpu.VMEM((4, 4, 64, 512), f32),
            pltpu.VMEM((4, 4, 64, 512), f32),
            pltpu.VMEM((32, 512), f32),
            pltpu.VMEM((16, 512), f32),
            pltpu.VMEM((16, 512), f32),
            pltpu.VMEM((TERMS, HALF, 128), f32),
            pltpu.VMEM((TERMS, 3 * SHARE[0], 128), f32),
            pltpu.VMEM((TERMS, 3 * SHARE[1], 128), f32),
            pltpu.VMEM((TERMS, 3 * SHARE[2], 128), f32),
            dma((4,)),
            dma((4,)),
            dma((2,)),
            dma((2,)),
            dma((2,)),
            dma((TERMS,)),
            dma((TERMS, 8)),
            dma((TERMS, 8)),
        ],
        compiler_params=pltpu.CompilerParams(
            vmem_limit_bytes=60 << 20, collective_id=0, has_side_effects=True
        ),
    )(
        die_basis,
        die_coeff.reshape(TERMS, 512),
        pkg_basis,
        send_blocks,
        columns,
        counts,
        pkg_blocks,
    )


def solution(mesh):
    placed = (
        P("gx", "gy", None),
        P(None, "gx", "gy"),
        P(("gx", "gy"), None, None),
        P(("gx", "gy"), None, None),
        P(None, ("gx", "gy"), None),
        P(None, ("gx", "gy")),
        P(None, ("gx", "gy"), None, None),
    )
    return jax.shard_map(body, mesh=mesh, in_specs=placed, out_specs=P(), check_vma=False)
```

time: 480 us -> 140 us (0.29); the launches traced: 472 us -> 139 us
  waiting for transfers between devices: 156 us -> 0 us
  matrix products: 131 us -> 0 us
  Pallas kernels: 0 us -> 131 us
  local copies, waits for them, and re-layouts: 132 us -> 8.7 us
  other arithmetic: 23.7 us -> 0 us
  starting transfers between devices: 15.3 us -> 0 us
  between operations: 13.9 us -> 0.01 us
    psum x1 -> x0, waiting for transfers between devices: 154 us -> none  [body(): return lax.psum(partial_terms, ('gx', 'gy'))]
    pallas_call x0 -> x1, Pallas kernels: none -> 131 us  [body(): pl.pallas_call(kernel, out_shape=jax.ShapeDtypeStruct((TERMS, 512, 512),...]
    dot_general x16 -> x0, matrix products: 131 us -> none  [the longest x5 68.5 us: package_terms(): image = jnp.einsum('rinj,rnjk->rik', matrices, picked, precision=highest)]
    gather x9 -> x0, local copies, waits for them, and re-layouts: 78.3 us -> none  [the longest x5 64 us: package_terms(): picked = table[columns[term_idx]]]
    another operation x5 -> x0, local copies, waits for them, and re-layouts: 23.5 us -> none  [package_terms(): blocks[term_idx].reshape(row_count, block, entries, block)]
    ppermute x6 -> x0, starting transfers between devices: 15.3 us -> none  [the longest x4 8.24 us: passed_along(): return lax.ppermute(value, axis, pairs)]
    mul x5 -> x0, other arithmetic: 14.7 us -> none  [package_terms(): blocks[term_idx].reshape(row_count, block, entries, block)]
    slice x5 -> x0, local copies, waits for them, and re-layouts: 8.19 us -> none  [the longest x1 7.95 us: package_terms(): blocks[term_idx].reshape(row_count, block, entries, block)]
  transfers between devices with their start and end apart: 7 -> 0, of which waited for: 2 -> 0; matrix products, arithmetic and copies ran while one was open for 17% -> 0% of each run, Pallas kernels for 0% -> 0%
where the time goes in v1:
time: 140 us; the launch traced here: 139 us
  Pallas kernels  131 us (94%)
  local copies, waits for them, and re-layouts  8.7 us (6%)
    pallas_call x1, Pallas kernels, body(): pl.pallas_call(kernel, out_shape=jax.ShapeDtypeStruct((TERMS, 512, 512),...  131 us
    unnamed x2, local copies, waits for them, and re-layouts  7.25 us

profile of v1, /device:TPU:1, one launch (start us, length us, event | category | flops | bytes accessed | tf_op | source)
XLA Modules:
  0.0 139.5 jit_solution(4634296445684336826)
XLA Ops:
  0.0 1.5 %reshape.3.coeff = f32[5,512]{1,0:T(8,128)} reshape(f32[5,16,32]{2,1,0:T(8,128)} %param.8) | data formatting | bytes 20480 | tf_op jit(solution)/shard_map/reshape | solution.py:355
  1.5 1.4 %copy.8.columns = s32[5,32,4]{2,1,0:T(8,128)} copy(s32[5,32,4]{1,2,0:T(4,128)} %param.11) | data formatting | bytes 5120 | tf_op args[4]
  2.9 130.8 %shard_map.73 = f32[5,512,512]{2,1,0:T(8,128)} custom-call(f32[16,32,512]{2,1,0:T(8,128)} %die.1, f32[5,512]{1,0:T(8,128)} %reshape.3.coeff, f32[32,64,512]{2,1,0:T(8,128)} %basis.1, s32[1,4,4]{2,1,0:T(4,128)} %lists.1, s32[5,32,4]{2,1,0:T(8,128)} %copy.8.columns, s32[5,32]{1,0:T(8,128)} %counts.1, f32[5,32,64,256]{3,2,1,0:T(8,128)} %blocks.1), custom_call_target="tpu_custom_call" | custom-call | tf_op jit(solution)/shard_map/pallas_call | solution.py:317
  133.7 5.8 %copy.10 = f32[5,512,512]{2,1,0:T(8,128)} copy(f32[5,512,512]{2,1,0:T(8,128)} %shard_map.73) | data formatting | bytes 10485760

commit v2 on v1

v2 whole, which is shorter than its diff:
```python
import jax
import jax.numpy as jnp
from jax import lax
from jax.experimental import pallas as pl
from jax.experimental.pallas import tpu as pltpu
from jax.sharding import PartitionSpec as P

MESH = pl.DeviceIdType.MESH
f32 = jnp.float32
bf16 = jnp.bfloat16
TERMS = 5
UNITS = 2 * TERMS
HALF = 512
SHARE = (128, 32, 8)
TURNS = (0, 1, 3, 4, 5, 6, 7, 9, 10)


def split(value):
    high = value.astype(bf16)
    low = (value - high.astype(f32)).astype(bf16)
    return high, low


def dot3(left, right):
    return jnp.dot(
        jnp.concatenate([left[0], left[1], left[0]], axis=1),
        jnp.concatenate([right[0], right[0], right[1]], axis=0),
        preferred_element_type=f32,
    )


def kernel(
    die, coeff, basis, lists, columns, counts, blocks, summed,
    table, basis_t, staged, image, field_t, field, share,
    ghost_out, ghost_in, row_in, col_out, col_in, got_core, got_0, got_1, got_2,
    ghost_send, ghost_recv, halo_send, halo_recv, stage_sem, send_sem, recv_sem,
):
    gx, gy = lax.axis_index("gx"), lax.axis_index("gy")
    core = lax.rem(gy, 2)
    spot = ((gx // 4) * 2 + lax.rem(gy // 2, 2), gy // 4, lax.rem(gx, 4))
    got = (got_0, got_1, got_2)

    def device_at(x, y, z, on_core):
        return ((x // 2) * 4 + z, y * 4 + lax.rem(x, 2) * 2 + on_core)

    def which(axis):
        return ((2 - axis) * (1 - axis) // 2, axis * (2 - axis), axis * (axis - 1) // 2)

    def along(axis, steps):
        x, y, z = (lax.rem(s + steps * w, 4) for s, w in zip(spot, which(axis)))
        return device_at(x, y, z, core)

    def place_on(axis):
        return sum(s * w for s, w in zip(spot, which(axis)))

    sibling = device_at(*spot, 1 - core)
    around = (
        (lax.rem(gx + 1, 8), gy),
        (lax.rem(gx + 7, 8), gy),
        (gx, lax.rem(gy + 1, 16)),
        (gx, lax.rem(gy + 15, 16)),
    )

    def stage_copy(unit, slot):
        return pltpu.make_async_copy(
            blocks.at[lax.rem(unit, TERMS)], staged.at[slot], stage_sem.at[slot]
        )

    stage_copy(0, 0).start()

    barrier = pltpu.get_barrier_semaphore()
    partners = [along(axis, steps) for axis in range(3) for steps in (1, 2, 3)]
    partners += [sibling, *around]
    for partner in partners:
        pl.semaphore_signal(barrier, inc=1, device_id=partner, device_id_type=MESH)
    pl.semaphore_wait(barrier, len(partners))

    def remote(source, target, send, recv, device):
        return pltpu.make_async_remote_copy(
            src_ref=source, dst_ref=target, send_sem=send, recv_sem=recv,
            device_id=device, device_id_type=MESH,
        )

    row_copy = remote(die.at[0], row_in, halo_send.at[0], halo_recv.at[0], around[1])
    row_copy.start()
    col_out[...] = die[:, 0, :]
    col_copy = remote(col_out, col_in, halo_send.at[1], halo_recv.at[1], around[3])
    col_copy.start()
    ghost_copies = []
    for part in range(2):
        for side in range(4):
            for slot in range(4):
                block = basis[lists[0, side, slot]]
                ghost_out[part, side, slot] = block[:, part * 256 : (part + 1) * 256]
            copy = remote(
                ghost_out.at[part, side], ghost_in.at[part, side],
                ghost_send.at[part, side], ghost_recv.at[part, side], around[side],
            )
            copy.start()
            ghost_copies.append(copy)

    def prepare(group, carry):
        value = basis[pl.ds(group * 4, 4)].reshape(256, 512)
        high, low = split(value)
        for part in range(2):
            lanes = slice(part * 256, (part + 1) * 256)
            table[part, pl.ds(group * 4, 4), :, :256] = high[:, lanes].reshape(4, 64, 256)
            table[part, pl.ds(group * 4, 4), :, 256:] = low[:, lanes].reshape(4, 64, 256)
        high, low = split(value.T)
        basis_t[group, 0] = high
        basis_t[group, 1] = low
        return carry

    lax.fori_loop(0, 8, prepare, 0)

    own = die[...]
    row_copy.wait()
    col_copy.wait()
    next_row = jnp.where(gx == 7, 0.0, row_in[...])
    next_col = jnp.where(gy == 15, 0.0, col_in[...])

    def keep_field(index, value):
        flat = value.reshape(512, 512)
        high, low = split(flat)
        field[index, 0] = high
        field[index, 1] = low
        field_t[index] = flat.T

    keep_field(0, own)
    keep_field(1, own - jnp.concatenate([own[1:], next_row[None]], axis=0))
    last = lax.broadcasted_iota(jnp.int32, (16, 32, 512), 1) == 31
    keep_field(2, own - jnp.where(last, next_col[:, None, :], jnp.roll(own, -1, axis=1)))
    share[...] = jnp.zeros_like(share)

    def die_term(step, carry):
        index = step // 2
        odd = lax.rem(step, 2)
        term = (1 - odd) * index + odd * (3 + (index + 1) // 2)
        fields = coeff[term]
        weights = jnp.concatenate([fields[row : row + 1] for row in range(16)], axis=1)
        weighted = split(field_t[index] * weights)
        gram = dot3(weighted, (field[index, 0], field[index, 1]))
        for lane in range(4):
            here = slice((lane % 2) * 512, (lane % 2 + 1) * 512)
            share[(lane // 2) * TERMS + term, here] += gram[:, lane * 128 : (lane + 1) * 128]
        return carry

    lax.fori_loop(0, 6, die_term, 0)

    def take_ghosts(part):
        for side in range(4):
            ghost_copies[part * 4 + side].wait()
            high, low = split(ghost_in[part, side])
            table[part, 32 + side * 4 : 36 + side * 4, :, :256] = high
            table[part, 32 + side * 4 : 36 + side * 4, :, 256:] = low

    take_ghosts(0)

    lane_at = lax.broadcasted_iota(jnp.int32, (64, 256), 1)

    def compute(unit):
        part, term, slot = unit // TERMS, lax.rem(unit, TERMS), lax.rem(unit, 2)
        stage_copy(unit, slot).wait()

        @pl.when(unit < UNITS - 1)
        def _():
            stage_copy(unit + 1, 1 - slot).start()

        def images(group, carry):
            for step in range(16):
                row = group * 16 + step
                kept = jnp.where(lane_at < counts[term, row] * 64, staged[slot, row], 0.0)
                both = jnp.dot(
                    jnp.concatenate(split(kept), axis=0),
                    jnp.concatenate(
                        [table[part, columns[term, entry, row]] for entry in range(4)], axis=0
                    ),
                    preferred_element_type=f32,
                )
                high, low = split(both[:64, :256] + both[64:, :256] + both[:64, 256:])
                here = pl.ds(pl.multiple_of(row * 64, 64), 64)
                image[0, here] = high
                image[1, here] = low
            return carry

        lax.fori_loop(0, 2, images, 0)
        highs = [basis_t[group, 0] for group in range(8)]
        lows = [basis_t[group, 1] for group in range(8)]
        product = jnp.dot(
            jnp.concatenate(highs + lows + highs, axis=1),
            jnp.concatenate([image[0], image[0], image[1]], axis=0),
            preferred_element_type=f32,
        )
        share[unit, :512] += product[:, :128]
        share[unit, 512:] += product[:, 128:]

    def offset(term, level):
        start = core * HALF
        for i in range(level):
            start = start + place_on(lax.rem(term + i, 3)) * SHARE[i]
        return pl.multiple_of(start, 8)

    def wait_bytes(ref, sem):
        pltpu.make_async_copy(ref, ref, sem).wait()

    def core_send(term):
        there = pl.multiple_of((1 - core) * HALF, 8)
        remote(
            share.at[term, pl.ds(there, HALF)], got_core.at[term],
            send_sem.at[term, 0], recv_sem.at[term, 0], sibling,
        ).start()

    def core_add(term):
        wait_bytes(got_core.at[term], recv_sem.at[term, 0])
        share[term, pl.ds(offset(term, 0), HALF)] += got_core[term]

    def scatter(term, level):
        axis, base, rows = lax.rem(term + level, 3), offset(term, level), SHARE[level]
        for steps in (1, 2, 3):
            there = pl.multiple_of(base + lax.rem(place_on(axis) + steps, 4) * rows, 8)
            remote(
                share.at[term, pl.ds(there, rows)],
                got[level].at[term, pl.ds((steps - 1) * rows, rows)],
                send_sem.at[term, 1 + level], recv_sem.at[term, 1 + level], along(axis, steps),
            ).start()

    def add(term, level, target):
        wait_bytes(got[level].at[term], recv_sem.at[term, 1 + level])
        rows, here = SHARE[level], pl.ds(offset(term, level + 1), SHARE[level])
        target[term, here] = (
            share[term, here]
            + got[level][term, :rows]
            + got[level][term, rows : 2 * rows]
            + got[level][term, 2 * rows :]
        )

    def gather(term, level):
        here = pl.ds(offset(term, level + 1), SHARE[level])
        axis = lax.rem(term + level, 3)
        for steps in (1, 2, 3):
            remote(
                summed.at[term, here], summed.at[term, here],
                send_sem.at[term, 4 + level], recv_sem.at[term, 4 + level], along(axis, steps),
            ).start()

    def gathered(term, level):
        wait_bytes(got[level].at[term], recv_sem.at[term, 4 + level])

    def core_gather(term):
        here = pl.ds(offset(term, 0), HALF)
        remote(
            summed.at[term, here], summed.at[term, here],
            send_sem.at[term, 7], recv_sem.at[term, 7], sibling,
        ).start()

    def close(term):
        wait_bytes(got_core.at[term], recv_sem.at[term, 7])

    def stage_0(term):
        core_send(term)

    def stage_1(term):
        core_add(term)
        scatter(term, 0)

    def stage_2(term):
        add(term, 0, share)
        scatter(term, 1)

    def stage_3(term):
        add(term, 1, share)
        scatter(term, 2)

    def stage_4(term):
        add(term, 2, summed)
        gather(term, 2)

    def stage_5(term):
        gathered(term, 2)
        gather(term, 1)

    def stage_6(term):
        gathered(term, 1)
        gather(term, 0)

    def stage_7(term):
        gathered(term, 0)
        core_gather(term)

    stages = (stage_0, stage_1, stage_2, stage_3, stage_4, stage_5, stage_6, stage_7, close)

    def turn(at, carry):
        @pl.when(at < UNITS)
        def _():
            @pl.when(at == TERMS)
            def _():
                take_ghosts(1)

            compute(at)

        for k in reversed(range(len(stages))):
            unit = at - TURNS[k]

            @pl.when((unit >= 0) & (unit < UNITS))
            def _(k=k, unit=unit):
                stages[k](unit)

        return carry

    lax.fori_loop(0, UNITS + TURNS[-1], turn, 0)

    def finish(term, carry):
        for k in (0, 7):
            wait_bytes(got_core.at[term], send_sem.at[term, k])
        for level in range(3):
            wait_bytes(got[level].at[term], send_sem.at[term, 1 + level])
            wait_bytes(got[level].at[term], send_sem.at[term, 4 + level])
        return carry

    lax.fori_loop(0, UNITS, finish, 0)


def lay_out(summed, out, sem):
    copies = []
    for unit in range(UNITS):
        for slab in range(2):
            column = (unit // TERMS) * 256 + slab * 128
            copies.append(
                pltpu.make_async_copy(
                    summed.at[unit, slab * 512 : (slab + 1) * 512],
                    out.at[unit % TERMS, :, column : column + 128],
                    sem.at[unit, slab],
                )
            )
    for copy in copies:
        copy.start()
    for copy in copies:
        copy.wait()


def body(die_basis, die_coeff, pkg_basis, send_blocks, columns, counts, pkg_blocks):
    vmem = pl.BlockSpec(memory_space=pltpu.VMEM)
    smem = pl.BlockSpec(memory_space=pltpu.SMEM)
    anywhere = pl.BlockSpec(memory_space=pl.ANY)
    dma = pltpu.SemaphoreType.DMA
    summed = pl.pallas_call(
        kernel,
        out_shape=pltpu.VMEM((UNITS, 2 * HALF, 128), f32),
        in_specs=[vmem, vmem, vmem, smem, smem, smem, anywhere],
        out_specs=vmem,
        scratch_shapes=[
            pltpu.VMEM((2, 48, 64, 512), bf16),
            pltpu.VMEM((8, 2, 512, 256), bf16),
            pltpu.VMEM((2, 32, 64, 256), f32),
            pltpu.VMEM((2, 2048, 256), bf16),
            pltpu.VMEM((3, 512, 512), f32),
            pltpu.VMEM((3, 2, 512, 512), bf16),
            pltpu.VMEM((UNITS, 2 * HALF, 128), f32),
            pltpu.VMEM((2, 4, 4, 64, 256), f32),
            pltpu.VMEM((2, 4, 4, 64, 256), f32),
            pltpu.VMEM((32, 512), f32),
            pltpu.VMEM((16, 512), f32),
            pltpu.VMEM((16, 512), f32),
            pltpu.VMEM((UNITS, HALF, 128), f32),
            pltpu.VMEM((UNITS, 3 * SHARE[0], 128), f32),
            pltpu.VMEM((UNITS, 3 * SHARE[1], 128), f32),
            pltpu.VMEM((UNITS, 3 * SHARE[2], 128), f32),
            dma((2, 4)),
            dma((2, 4)),
            dma((2,)),
            dma((2,)),
            dma((2,)),
            dma((UNITS, 8)),
            dma((UNITS, 8)),
        ],
        compiler_params=pltpu.CompilerParams(
            vmem_limit_bytes=56 << 20, collective_id=0, has_side_effects=True
        ),
    )(
        die_basis,
        die_coeff,
        pkg_basis,
        send_blocks,
        jnp.transpose(columns, (0, 2, 1)),
        counts,
        pkg_blocks,
    )
    return pl.pallas_call(
        lay_out,
        out_shape=jax.ShapeDtypeStruct((TERMS, 512, 512), f32),
        in_specs=[anywhere],
        out_specs=anywhere,
        scratch_shapes=[dma((UNITS, 2))],
        compiler_params=pltpu.CompilerParams(vmem_limit_bytes=1 << 20),
    )(summed)


def solution(mesh):
    placed = (
        P("gx", "gy", None),
        P(None, "gx", "gy"),
        P(("gx", "gy"), None, None),
        P(("gx", "gy"), None, None),
        P(None, ("gx", "gy"), None),
        P(None, ("gx", "gy")),
        P(None, ("gx", "gy"), None, None),
    )
    return jax.shard_map(body, mesh=mesh, in_specs=placed, out_specs=P(), check_vma=False)
```

time: 140 us -> 103 us (0.74)
  Pallas kernels: 131 us -> 103 us
  local copies, waits for them, and re-layouts: 8.7 us -> 0 us
    pallas_call x1 -> x2, Pallas kernels: 131 us -> 103 us  [the longest x1 101 us: body(): pl.pallas_call(kernel, out_shape=pltpu.VMEM((UNITS, 2 * HALF, 128), f32),...]
    unnamed x2 -> x0, local copies, waits for them, and re-layouts: 7.25 us -> none
    reshape x1 -> x0, local copies, waits for them, and re-layouts: 1.46 us -> none  [body(): die_coeff.reshape(TERMS, 512)]
where the time goes in v2:
time: 103 us
  Pallas kernels  103 us (100%)
    pallas_call x1, Pallas kernels, body(): pl.pallas_call(kernel, out_shape=pltpu.VMEM((UNITS, 2 * HALF, 128), f32),...  101 us
    pallas_call x1, Pallas kernels, body(): pl.pallas_call(lay_out, out_shape=jax.ShapeDtypeStruct((TERMS, 512, 512),...  2.49 us

profile of v2, /device:TPU:1, one launch (start us, length us, event | category | flops | bytes accessed | tf_op | source)
XLA Modules:
  0.0 103.0 jit_solution(6409933983602103133)
XLA Ops:
  0.0 100.5 %shard_map.73.summed = f32[10,1024,128]{2,1,0:T(8,128)S(1)} custom-call(f32[16,32,512]{2,1,0:T(8,128)} %die.1, f32[5,16,32]{2,1,0:T(8,128)} %coeff.1, f32[32,64,512]{2,1,0:T(8,128)} %basis.1, s32[1,4,4]{2,1,0:T(4,128)} %lists.1, s32[5,4,32]{2,1,0:T(4,128)} %bitcast.1, s32[5,32]{1,0:T(8,128)} %counts.1, f32[5,32,64,256]{3,2,1,0:T(8,128)} %blocks.1), custom_call_target="tpu_custom_call" | custom-call | tf_op jit(solution)/shard_map/pallas_call | solution.py:346
  100.5 2.5 %shard_map.74 = f32[5,512,512]{2,1,0:T(8,128)} custom-call(f32[10,1024,128]{2,1,0:T(8,128)S(1)} %shard_map.73.summed), custom_call_target="tpu_custom_call" | custom-call | tf_op jit(solution)/shard_map/pallas_call | solution.py:388

commit v3 on v2

--- a/solution.py
+++ b/solution.py
@@ -13,6 +13,9 @@
 HALF = 512
 SHARE = (128, 32, 8)
 TURNS = (0, 1, 3, 4, 5, 6, 7, 9, 10)
+EARLY = 3
+PLANE = 7
+OTHERS = [(i, j) for i in range(4) for j in range(4) if (i, j) != (0, 0)]
 
 
 def split(value):
@@ -32,7 +35,7 @@
 def kernel(
     die, coeff, basis, lists, columns, counts, blocks, summed,
     table, basis_t, staged, image, field_t, field, share,
-    ghost_out, ghost_in, row_in, col_out, col_in, got_core, got_0, got_1, got_2,
+    ghost_out, ghost_in, row_in, col_out, col_in, got_core, got_0, got_1, got_2, got_plane,
     ghost_send, ghost_recv, halo_send, halo_recv, stage_sem, send_sem, recv_sem,
 ):
     gx, gy = lax.axis_index("gx"), lax.axis_index("gy")
@@ -52,6 +55,11 @@
 
     def place_on(axis):
         return sum(s * w for s, w in zip(spot, which(axis)))
+
+    def across(unit, i, j):
+        steps = [0, 0, 0]
+        steps[(unit + 1) % 3], steps[(unit + 2) % 3] = i, j
+        return device_at(*(lax.rem(s + n, 4) for s, n in zip(spot, steps)), core)
 
     sibling = device_at(*spot, 1 - core)
     around = (
@@ -70,6 +78,8 @@
 
     barrier = pltpu.get_barrier_semaphore()
     partners = [along(axis, steps) for axis in range(3) for steps in (1, 2, 3)]
+    for unit in range(PLANE, UNITS):
+        partners += [across(unit, i, j) for i, j in OTHERS if i and j]
     partners += [sibling, *around]
     for partner in partners:
         pl.semaphore_signal(barrier, inc=1, device_id=partner, device_id_type=MESH)
@@ -289,25 +299,70 @@
 
     stages = (stage_0, stage_1, stage_2, stage_3, stage_4, stage_5, stage_6, stage_7, close)
 
+    def plane_scatter(unit):
+        add(unit, 0, share)
+        base = offset(unit, 1)
+        first, second = spot[(unit + 1) % 3], spot[(unit + 2) % 3]
+        for slot, (i, j) in enumerate(OTHERS):
+            there = base + lax.rem(first + i, 4) * 32 + lax.rem(second + j, 4) * 8
+            remote(
+                share.at[unit, pl.ds(pl.multiple_of(there, 8), 8)],
+                got_plane.at[unit - PLANE, pl.ds(slot * 8, 8)],
+                send_sem.at[unit, 2], recv_sem.at[unit, 2], across(unit, i, j),
+            ).start()
+
+    def plane_gather(unit):
+        wait_bytes(got_plane.at[unit - PLANE], recv_sem.at[unit, 2])
+        here = pl.ds(offset(unit, 3), 8)
+        tile = share[unit, here]
+        for slot in range(15):
+            tile = tile + got_plane[unit - PLANE, slot * 8 : (slot + 1) * 8]
+        summed[unit, here] = tile
+        for i, j in OTHERS:
+            remote(
+                summed.at[unit, here], summed.at[unit, here],
+                send_sem.at[unit, 5], recv_sem.at[unit, 5], across(unit, i, j),
+            ).start()
+
+    def plane_gathered(unit):
+        wait_bytes(got_plane.at[unit - PLANE], recv_sem.at[unit, 5])
+        gather(unit, 0)
+
+    short = (stage_0, stage_1, plane_scatter, plane_gather, plane_gathered, stage_7, close)
+
     def turn(at, carry):
-        @pl.when(at < UNITS)
+        @pl.when(at == TERMS)
         def _():
-            @pl.when(at == TERMS)
-            def _():
-                take_ghosts(1)
-
-            compute(at)
-
+            take_ghosts(1)
+
+        compute(at)
         for k in reversed(range(len(stages))):
-            unit = at - TURNS[k]
-
-            @pl.when((unit >= 0) & (unit < UNITS))
-            def _(k=k, unit=unit):
-                stages[k](unit)
+            if k < EARLY:
+                unit = at - TURNS[k]
+                last = UNITS if k < 2 else PLANE
+
+                @pl.when((unit >= 0) & (unit < last))
+                def _(k=k, unit=unit):
+                    stages[k](unit)
 
         return carry
 
-    lax.fori_loop(0, UNITS + TURNS[-1], turn, 0)
+    lax.fori_loop(0, UNITS, turn, 0)
+
+    left = {}
+    for unit in range(UNITS):
+        steps = stages if unit < PLANE else short
+        at = 0
+        for k, stage in enumerate(steps):
+            in_loop = k < EARLY and unit + TURNS[k] < UNITS and (k < 2 or unit < PLANE)
+            at = unit + TURNS[k] if in_loop else max(at + 1, UNITS)
+            if stage in (stage_7, close):
+                at = max(at, 2 * UNITS)
+            if not in_loop:
+                left.setdefault(at, []).append((k, unit, stage))
+    for at in sorted(left):
+        for k, unit, stage in sorted(left[at], key=lambda entry: entry[1]):
+            stage(unit)
 
     def finish(term, carry):
         for k in (0, 7):
@@ -317,7 +372,14 @@
             wait_bytes(got[level].at[term], send_sem.at[term, 4 + level])
         return carry
 
-    lax.fori_loop(0, UNITS, finish, 0)
+    lax.fori_loop(0, PLANE, finish, 0)
+    for unit in range(PLANE, UNITS):
+        for k in (0, 7):
+            wait_bytes(got_core.at[unit], send_sem.at[unit, k])
+        for k in (1, 4):
+            wait_bytes(got_0.at[unit], send_sem.at[unit, k])
+        for k in (2, 5):
+            wait_bytes(got_plane.at[unit - PLANE], send_sem.at[unit, k])
 
 
 def lay_out(summed, out, sem):
@@ -365,6 +427,7 @@
             pltpu.VMEM((UNITS, 3 * SHARE[0], 128), f32),
             pltpu.VMEM((UNITS, 3 * SHARE[1], 128), f32),
             pltpu.VMEM((UNITS, 3 * SHARE[2], 128), f32),
+            pltpu.VMEM((UNITS - PLANE, 120, 128), f32),
             dma((2, 4)),
             dma((2, 4)),
             dma((2,)),

time: 103 us -> 97.2 us (0.944)
  Pallas kernels: 103 us -> 97.1 us
    pallas_call x1, Pallas kernels: 101 us -> 94.6 us  [body(): pl.pallas_call(kernel, out_shape=pltpu.VMEM((UNITS, 2 * HALF, 128), f32),...]
where the time goes in v3:
time: 97.2 us; the launch traced here: 97.1 us
  Pallas kernels  97.1 us (100%)
    pallas_call x1, Pallas kernels, body(): pl.pallas_call(kernel, out_shape=pltpu.VMEM((UNITS, 2 * HALF, 128), f32),...  94.6 us
    pallas_call x1, Pallas kernels, body(): pl.pallas_call(lay_out, out_shape=jax.ShapeDtypeStruct((TERMS, 512, 512),...  2.49 us

profile of v3, /device:TPU:1, one launch (start us, length us, event | category | flops | bytes accessed | tf_op | source)
XLA Modules:
  0.0 97.1 jit_solution(5247344409838205330)
XLA Ops:
  0.0 94.6 %shard_map.73.summed = f32[10,1024,128]{2,1,0:T(8,128)S(1)} custom-call(f32[16,32,512]{2,1,0:T(8,128)} %die.1, f32[5,16,32]{2,1,0:T(8,128)} %coeff.1, f32[32,64,512]{2,1,0:T(8,128)} %basis.1, s32[1,4,4]{2,1,0:T(4,128)} %lists.1, s32[5,4,32]{2,1,0:T(4,128)} %bitcast.1, s32[5,32]{1,0:T(8,128)} %counts.1, f32[5,32,64,256]{3,2,1,0:T(8,128)} %blocks.1), custom_call_target="tpu_custom_call" | custom-call | tf_op jit(solution)/shard_map/pallas_call | solution.py:408
  94.6 2.5 %shard_map.74 = f32[5,512,512]{2,1,0:T(8,128)} custom-call(f32[10,1024,128]{2,1,0:T(8,128)S(1)} %shard_map.73.summed), custom_call_target="tpu_custom_call" | custom-call | tf_op jit(solution)/shard_map/pallas_call | solution.py:451

commit v4 on v3

--- a/solution.py
+++ b/solution.py
@@ -176,24 +176,19 @@
         def _():
             stage_copy(unit + 1, 1 - slot).start()
 
-        def images(group, carry):
-            for step in range(16):
-                row = group * 16 + step
-                kept = jnp.where(lane_at < counts[term, row] * 64, staged[slot, row], 0.0)
-                both = jnp.dot(
-                    jnp.concatenate(split(kept), axis=0),
-                    jnp.concatenate(
-                        [table[part, columns[term, entry, row]] for entry in range(4)], axis=0
-                    ),
-                    preferred_element_type=f32,
-                )
-                high, low = split(both[:64, :256] + both[64:, :256] + both[:64, 256:])
-                here = pl.ds(pl.multiple_of(row * 64, 64), 64)
-                image[0, here] = high
-                image[1, here] = low
-            return carry
-
-        lax.fori_loop(0, 2, images, 0)
+        for row in range(32):
+            kept = jnp.where(lane_at < counts[term, row] * 64, staged[slot, row], 0.0)
+            both = jnp.dot(
+                jnp.concatenate(split(kept), axis=0),
+                jnp.concatenate(
+                    [table[part, columns[term, entry, row]] for entry in range(4)], axis=0
+                ),
+                preferred_element_type=f32,
+            )
+            high, low = split(both[:64, :256] + both[64:, :256] + both[:64, 256:])
+            here = slice(row * 64, (row + 1) * 64)
+            image[0, here] = high
+            image[1, here] = low
         highs = [basis_t[group, 0] for group in range(8)]
         lows = [basis_t[group, 1] for group in range(8)]
         product = jnp.dot(

time: 97.2 us -> 94.5 us (0.972)
  Pallas kernels: 97.1 us -> 94.4 us
    pallas_call x1, Pallas kernels: 94.6 us -> 91.9 us  [body(): pl.pallas_call(kernel, out_shape=pltpu.VMEM((UNITS, 2 * HALF, 128), f32),...]
where the time goes in v4:
time: 94.5 us; the launch traced here: 94.4 us
  Pallas kernels  94.4 us (100%)
    pallas_call x1, Pallas kernels, body(): pl.pallas_call(kernel, out_shape=pltpu.VMEM((UNITS, 2 * HALF, 128), f32),...  91.9 us
    pallas_call x1, Pallas kernels, body(): pl.pallas_call(lay_out, out_shape=jax.ShapeDtypeStruct((TERMS, 512, 512),...  2.49 us

profile of v4, /device:TPU:1, one launch (start us, length us, event | category | flops | bytes accessed | tf_op | source)
XLA Modules:
  0.0 94.4 jit_solution(17081329788235665656)
XLA Ops:
  0.0 91.9 %shard_map.73.summed = f32[10,1024,128]{2,1,0:T(8,128)S(1)} custom-call(f32[16,32,512]{2,1,0:T(8,128)} %die.1, f32[5,16,32]{2,1,0:T(8,128)} %coeff.1, f32[32,64,512]{2,1,0:T(8,128)} %basis.1, s32[1,4,4]{2,1,0:T(4,128)} %lists.1, s32[5,4,32]{2,1,0:T(4,128)} %bitcast.1, s32[5,32]{1,0:T(8,128)} %counts.1, f32[5,32,64,256]{3,2,1,0:T(8,128)} %blocks.1), custom_call_target="tpu_custom_call" | custom-call | tf_op jit(solution)/shard_map/pallas_call | solution.py:403
  91.9 2.5 %shard_map.74 = f32[5,512,512]{2,1,0:T(8,128)} custom-call(f32[10,1024,128]{2,1,0:T(8,128)S(1)} %shard_map.73.summed), custom_call_target="tpu_custom_call" | custom-call | tf_op jit(solution)/shard_map/pallas_call | solution.py:446
